TPU v7x, 32 devices: a whole 2x2x4 slice. The times are simulated.
32 devices in a mesh: inp: 4 (over z), out: 4 (over y, core), dep: 2 (over x).
Axes of the slice: x: 2, y: 2, z: 4, core: 2. Of those that a mesh axis runs over, the one named last changes fastest.
Arguments:
- tokens: bfloat16 [384, 8192], P('dep', 'inp'), may hold values from -6 to 6
- grad_hidden: bfloat16 [384, 14336], P('dep', 'out'), may hold values from -3 to 3
- w_gate: bfloat16 [8192, 14336], P('inp', 'out'), may hold values from -0.0625 to 0.0625
- w_up: bfloat16 [8192, 14336], P('inp', 'out'), may hold values from -0.0625 to 0.0625
Outputs:
- grad_input: bfloat16 [384, 8192], P('dep', ('inp', 'out'))
- gate_grad: bfloat16 [8192, 14336], P(('inp', 'dep'), 'out')
- up_grad: bfloat16 [8192, 14336], P(('inp', 'dep'), 'out')
All inputs are finite; a program needn't handle non-finite values.
Results may differ from a plain program's by a relative error of at most 0.019.
Values may be sent and summed in bfloat16 or wider, within the bound.
A program may use at most 128 MiB of HBM per device.

v0:
```python
import math

import jax
import jax.numpy as jnp
from jax import lax
from jax.sharding import PartitionSpec as P


def local_product(left, right):
    return jnp.dot(left, right, preferred_element_type=jnp.float32)


def contract_rows(left, right):
    return lax.dot_general(
        left, right, (((0,), (0,)), ((), ())), preferred_element_type=jnp.float32
    )


def contract_cols(left, right):
    return lax.dot_general(
        left, right, (((1,), (1,)), ((), ())), preferred_element_type=jnp.float32
    )


def shards(tokens, grad_hidden, w_gate, w_up):
    token_count = tokens.shape[0]
    own_rows = token_count // lax.axis_size("inp")
    hidden_width = w_gate.shape[1]
    factor = 1.0 / math.sqrt(token_count * lax.axis_size("dep"))
    summed = lax.psum_scatter(
        jnp.concatenate([local_product(tokens, w_gate), local_product(tokens, w_up)], axis=1),
        "inp",
        scatter_dimension=0,
        tiled=True,
    )
    gate_value = summed[:, :hidden_width]
    up_value = summed[:, hidden_width:]
    offset = lax.axis_index("inp") * own_rows
    cotangent = lax.dynamic_slice_in_dim(grad_hidden, offset, own_rows, 0).astype(jnp.float32)
    sigmoid_gate = jax.nn.sigmoid(gate_value)
    grad_gate = (
        cotangent * up_value * sigmoid_gate * (1.0 + gate_value * (1.0 - sigmoid_gate))
    ).astype(jnp.bfloat16)
    grad_upper = (cotangent * gate_value * sigmoid_gate).astype(jnp.bfloat16)
    paired = jnp.concatenate([grad_gate, grad_upper], axis=1)
    gathered = lax.all_gather(paired, "inp", axis=0, tiled=True)
    full_gate = gathered[:, :hidden_width]
    full_upper = gathered[:, hidden_width:]
    input_terms = contract_cols(full_gate, w_gate) + contract_cols(full_upper, w_up)
    grad_input = lax.psum_scatter(input_terms, "out", scatter_dimension=1, tiled=True).astype(
        jnp.bfloat16
    )
    gate_part = contract_rows(tokens, full_gate)
    upper_part = contract_rows(tokens, full_upper)
    gate_sum, upper_sum = (
        lax.psum_scatter(
            gate_part.astype(jnp.bfloat16), "dep", scatter_dimension=0, tiled=True
        ).astype(jnp.float32),
        lax.psum_scatter(
            upper_part.astype(jnp.bfloat16), "dep", scatter_dimension=0, tiled=True
        ).astype(jnp.float32),
    )
    return (
        grad_input,
        (gate_sum * factor).astype(jnp.bfloat16),
        (upper_sum * factor).astype(jnp.bfloat16),
    )


def solution(mesh):
    return jax.shard_map(
        shards,
        mesh=mesh,
        in_specs=(P("dep", "inp"), P("dep", "out"), P("inp", "out"), P("inp", "out")),
        out_specs=(P("dep", ("inp", "out")), P(("inp", "dep"), "out"), P(("inp", "dep"), "out")),
        check_vma=False,
    )
```

profile of v0, /device:TPU:0, one launch (start us, length us, event | category | flops | bytes accessed | tf_op | source)
XLA Modules:
  0.0 595.2 jit_solution(2465058671951119493)
XLA Ops:
  7.2 1.1 copy-done
  8.3 6.9 %fusion.12 = f32[192,3584]{1,0:T(8,128)S(1)} fusion(bf16[192,2048]{1,0:T(8,128)(2,1)S(1)} %copy-done, bf16[2048,3584]{1,0:T(8,128)(2,1)} %param.6), kind=kOutput, calls=%fused_computation.22 | convolution fusion | flops 2818572288 | bytes 18219008 | tf_op jit(solution)/shard_map/dot_general | solution.py:10
  15.2 2.4 copy-done.2
  17.7 3.1 fusion.13
  20.7 2.9 pad_maximum_fusion
  23.6 0.0 all-gather.2.cloned.1.call-start
  23.7 100.8 %reduce-scatter.5.cloned.1.call-done = f32[48,7168]{1,0:T(8,128)} async-done(((f32[192,7168]{1,0:T(8,128)}), f32[48,7168]{1,0:T(8,128)}) %reduce-scatter.5.cloned.1.call-update) | async-done | bytes 1376272 | tf_op jit(solution)/shard_map/reduce_scatter | solution.py:30
  124.5 1.7 fusion.9
  126.2 0.9 pad_maximum_fusion.1
  127.1 0.0 reduce-scatter.7.cloned.1.call-start
  127.2 57.6 %all-gather.2.cloned.1.call-done = bf16[192,7168]{1,0:T(8,128)(2,1)} async-done(((bf16[48,7168]{1,0:T(8,128)(2,1)}), bf16[192,7168]{1,0:T(8,128)(2,1)}) %all-gather.2.cloned.1.call-update) | async-done | bytes 2752528 | tf_op jit(solution)/shard_map/all_gather | solution.py:46
  184.8 8.6 %fusion.5 = f32[192,2048]{1,0:T(8,128)S(1)} fusion(bf16[2048,3584]{1,0:T(8,128)(2,1)} %param.6, bf16[192,7168]{1,0:T(8,128)(2,1)} %all-gather.2.cloned.1.call-done), kind=kOutput, calls=%fused_computation.11 | convolution fusion | flops 2818572288 | bytes 17629184 | tf_op jit(solution)/shard_map/dot_general | solution.py:20
  193.4 11.2 %convolution_add_fusion = f32[192,2048]{1,0:T(8,128)} fusion(f32[192,2048]{1,0:T(8,128)S(1)} %fusion.5, bf16[2048,3584]{1,0:T(8,128)(2,1)} %param.7, bf16[192,7168]{1,0:T(8,128)(2,1)S(1)} %copy-done.1), kind=kOutput, calls=%fused_computation.7 | convolution fusion | flops 2818965504 | bytes 19202048 | tf_op jit(solution)/shard_map/dot_general | solution.py:20
  204.7 7.6 %fusion = bf16[2048,3584]{0,1:T(8,128)(2,1)} fusion(bf16[192,2048]{1,0:T(8,128)(2,1)S(1)} %copy-done, bf16[192,7168]{1,0:T(8,128)(2,1)S(1)} %copy-done.1), kind=kOutput, calls=%fused_computation.4 | convolution fusion | flops 2825912320 | bytes 16842752 | tf_op jit(solution)/shard_map/dot_general | solution.py:14
  212.3 0.2 reduce-scatter.11.cloned.1.call-start
  212.5 7.3 %fusion.1 = bf16[2048,3584]{0,1:T(8,128)(2,1)} fusion(bf16[192,2048]{1,0:T(8,128)(2,1)S(1)} %copy-done, bf16[192,7168]{1,0:T(8,128)(2,1)S(1)} %copy-done.1), kind=kOutput, calls=%fused_computation.5 | convolution fusion | flops 2825912320 | bytes 16842752 | tf_op jit(solution)/shard_map/dot_general | solution.py:14
  219.9 11.9 %reduce-scatter.7.cloned.1.call-done = f32[192,512]{1,0:T(8,128)} async-done(((f32[192,2048]{1,0:T(8,128)}), f32[192,512]{1,0:T(8,128)}) %reduce-scatter.7.cloned.1.call-update) | async-done | bytes 393232 | tf_op jit(solution)/shard_map/reduce_scatter | solution.py:50
  231.7 1.7 convert_element_type.39
  233.4 167.7 %reduce-scatter.9.cloned.1.call-done = bf16[1024,3584]{0,1:T(8,128)(2,1)} async-done(((bf16[2048,3584]{0,1:T(8,128)(2,1)}), bf16[1024,3584]{0,1:T(8,128)(2,1)}) %reduce-scatter.9.cloned.1.call-update) | async-done | bytes 7340048 | tf_op jit(solution)/shard_map/reduce_scatter | solution.py:56
  401.1 8.3 %multiply_convert_fusion.1 = bf16[1024,3584]{0,1:T(8,128)(2,1)} fusion(bf16[1024,3584]{0,1:T(8,128)(2,1)} %reduce-scatter.9.cloned.1.call-done), kind=kLoop, calls=%fused_computation.3 | loop fusion | flops 11010048 | bytes 14680064 | tf_op jit(solution)/shard_map/convert_element_type | solution.py:65
  409.5 10.2 %copy.7 = bf16[1024,3584]{1,0:T(8,128)(2,1)} copy(bf16[1024,3584]{0,1:T(8,128)(2,1)} %multiply_convert_fusion.1) | data formatting | bytes 14680064
  419.6 150.8 %reduce-scatter.11.cloned.1.call-done = bf16[1024,3584]{0,1:T(8,128)(2,1)} async-done(((bf16[2048,3584]{0,1:T(8,128)(2,1)}), bf16[1024,3584]{0,1:T(8,128)(2,1)}) %reduce-scatter.11.cloned.1.call-update) | async-done | bytes 7340048 | tf_op jit(solution)/shard_map/reduce_scatter | solution.py:59
  570.5 8.2 %multiply_convert_fusion = bf16[1024,3584]{0,1:T(8,128)(2,1)} fusion(bf16[1024,3584]{0,1:T(8,128)(2,1)} %reduce-scatter.11.cloned.1.call-done), kind=kLoop, calls=%fused_computation.2 | loop fusion | flops 11010048 | bytes 14680064 | tf_op jit(solution)/shard_map/convert_element_type | solution.py:66
  578.7 9.9 %copy.8 = bf16[1024,3584]{1,0:T(8,128)(2,1)} copy(bf16[1024,3584]{0,1:T(8,128)(2,1)} %multiply_convert_fusion) | data formatting | bytes 14680064
  (11 shorter events, 0.2 us)
Async XLA Ops:
  7.2 1.1 copy-start
  7.2 117.3 %reduce-scatter.5.cloned.1.call-start = ((), (), s32[]{:S(2)}) async-start(), calls=%async_computation.4 | async-start | bytes 6881280 | tf_op jit(solution)/shard_map/reduce_scatter | solution.py:30
  8.3 9.3 %copy-start.2 = (bf16[2048,3584]{1,0:T(8,128)(2,1)S(1)}, bf16[2048,3584]{1,0:T(8,128)(2,1)}, u32[]{:S(2)}) copy-start(bf16[2048,3584]{1,0:T(8,128)(2,1)} %param.7) | copy-start | bytes 44040196
  23.6 161.1 %all-gather.2.cloned.1.call-start = ((), (), s32[]{:S(2)}) async-start(), calls=%async_computation.5 | async-start | bytes 3440640 | tf_op jit(solution)/shard_map/all_gather | solution.py:46
  127.1 104.6 %reduce-scatter.7.cloned.1.call-start = ((), (), s32[]{:S(2)}) async-start(), calls=%async_computation.6 | async-start | bytes 1966080 | tf_op jit(solution)/shard_map/reduce_scatter | solution.py:50
  184.8 8.6 %copy-start.1 = (bf16[192,7168]{1,0:T(8,128)(2,1)S(1)}, bf16[192,7168]{1,0:T(8,128)(2,1)}, u32[]{:S(2)}) copy-start(bf16[192,7168]{1,0:T(8,128)(2,1)} %all-gather.2.cloned.1.call-done) | copy-start | bytes 8257540
  204.7 196.5 %reduce-scatter.9.cloned.1.call-start = ((), (), s32[]{:S(2)}) async-start(), calls=%async_computation.7 | async-start | bytes 22020096 | tf_op jit(solution)/shard_map/reduce_scatter | solution.py:56
  212.3 358.2 %reduce-scatter.11.cloned.1.call-start = ((), (), s32[]{:S(2)}) async-start(), calls=%async_computation.8 | async-start | bytes 22020096 | tf_op jit(solution)/shard_map/reduce_scatter | solution.py:59
Sparse Core Ops, SparseCore 0:
  23.8 100.6 reduce-scatter.4
  127.2 57.4 all-gather.1
  204.8 26.9 reduce-scatter.6
  234.0 167.0 reduce-scatter.8
  403.4 167.0 reduce-scatter.10
where the time goes:
time: 596 us; the launch traced here: 595 us
  waiting for transfers between devices  489 us (82%)
  matrix products  44.7 us (8%)
  other arithmetic  23.8 us (4%)
  local copies, waits for them, and re-layouts  23.6 us (4%)
  between operations  13.8 us (2%)
    reduce_scatter x1, waiting for transfers between devices, shards(): lax.psum_scatter(gate_part.astype(jnp.bfloat16), 'dep', scatter_dimension...  168 us
    reduce_scatter x1, waiting for transfers between devices, shards(): lax.psum_scatter(upper_part.astype(jnp.bfloat16), 'dep', scatter_dimensio...  151 us
    reduce_scatter x1, waiting for transfers between devices, shards(): lax.psum_scatter(jnp.concatenate([local_product(tokens, w_gate), local_pr...  101 us
    all_gather x1, waiting for transfers between devices, shards(): gathered = lax.all_gather(paired, 'inp', axis=0, tiled=True)  57.6 us
    unnamed x8, local copies, waits for them, and re-layouts  23.6 us
    dot_general x2, matrix products, contract_cols(): lax.dot_general(left, right, (((1,), (1,)), ((), ())), preferred_element_...  19.8 us
    dot_general x2, matrix products, contract_rows(): lax.dot_general(left, right, (((0,), (0,)), ((), ())), preferred_element_...  14.9 us
  transfers between devices with their start and end apart: 5, of which 5 were waited for; matrix products, arithmetic and copies ran while one was open for 6% of the time, Pallas kernels for 0%

commit v1 on v0

--- a/solution.py
+++ b/solution.py
@@ -28,11 +28,14 @@
     hidden_width = w_gate.shape[1]
     factor = 1.0 / math.sqrt(token_count * lax.axis_size("dep"))
     summed = lax.psum_scatter(
-        jnp.concatenate([local_product(tokens, w_gate), local_product(tokens, w_up)], axis=1),
+        jnp.concatenate(
+            [local_product(tokens, w_gate), local_product(tokens, w_up)], axis=1
+        ).astype(jnp.bfloat16),
         "inp",
         scatter_dimension=0,
         tiled=True,
     )
+    summed = summed.astype(jnp.float32)
     gate_value = summed[:, :hidden_width]
     up_value = summed[:, hidden_width:]
     offset = lax.axis_index("inp") * own_rows
@@ -50,21 +53,15 @@
     grad_input = lax.psum_scatter(input_terms, "out", scatter_dimension=1, tiled=True).astype(
         jnp.bfloat16
     )
-    gate_part = contract_rows(tokens, full_gate)
-    upper_part = contract_rows(tokens, full_upper)
-    gate_sum, upper_sum = (
-        lax.psum_scatter(
-            gate_part.astype(jnp.bfloat16), "dep", scatter_dimension=0, tiled=True
-        ).astype(jnp.float32),
-        lax.psum_scatter(
-            upper_part.astype(jnp.bfloat16), "dep", scatter_dimension=0, tiled=True
-        ).astype(jnp.float32),
+    dep_count = lax.axis_size("dep")
+    every_token = lax.all_gather(tokens, "dep", axis=0, tiled=True)
+    own_features = tokens.shape[1] // dep_count
+    own_tokens = lax.dynamic_slice_in_dim(
+        every_token, lax.axis_index("dep") * own_features, own_features, 1
     )
-    return (
-        grad_input,
-        (gate_sum * factor).astype(jnp.bfloat16),
-        (upper_sum * factor).astype(jnp.bfloat16),
-    )
+    every_grad = lax.all_gather(gathered, "dep", axis=0, tiled=True)
+    weight_grad = (contract_rows(own_tokens, every_grad) * factor).astype(jnp.bfloat16)
+    return grad_input, weight_grad[:, :hidden_width], weight_grad[:, hidden_width:]
 
 
 def solution(mesh):

time: 596 us -> 284 us (0.48)
  waiting for transfers between devices: 489 us -> 213 us
  local copies, waits for them, and re-layouts: 23.6 us -> 6.73 us
  other arithmetic: 23.8 us -> 6.96 us
    reduce_scatter x2 -> x0, waiting for transfers between devices: 319 us -> none  [the longest x1 168 us: shards(): lax.psum_scatter(gate_part.astype(jnp.bfloat16), 'dep', scatter_dimension...]
    all_gather x0 -> x2, waiting for transfers between devices: none -> 72 us  [the longest x1 72 us: shards(): every_grad = lax.all_gather(gathered, 'dep', axis=0, tiled=True)]
    reduce_scatter x1, waiting for transfers between devices: 101 us -> 56.9 us  [shards(): lax.psum_scatter(jnp.concatenate([local_product(tokens, w_gate), local_pr...]
    unnamed x8 -> x6, local copies, waits for them, and re-layouts: 23.6 us -> 1.22 us
    convert_element_type x2 -> x1, other arithmetic: 16.6 us -> 1.19 us  [shards(): summed = summed.astype(jnp.float32)]
    reduce_scatter x1, waiting for transfers between devices: 11.9 us -> 25.9 us  [shards(): lax.psum_scatter(input_terms, 'out', scatter_dimension=1, tiled=True)]
    dot_general x2 -> x1, matrix products: 14.9 us -> 10 us  [contract_rows(): lax.dot_general(left, right, (((0,), (0,)), ((), ())), preferred_element_...]
  transfers between devices with their start and end apart: 5 -> 5, of which waited for: 5 -> 4; matrix products, arithmetic and copies ran while one was open for 6% -> 1% of each run, Pallas kernels for 0% -> 0%
where the time goes in v1:
time: 284 us; the launch traced here: 283 us
  waiting for transfers between devices  213 us (75%)
  matrix products  41.5 us (15%)
  between operations  15.3 us (5%)
  other arithmetic  6.96 us (2%)
  local copies, waits for them, and re-layouts  6.73 us (2%)
    all_gather x1, waiting for transfers between devices, shards(): every_grad = lax.all_gather(gathered, 'dep', axis=0, tiled=True)  72 us
    reduce_scatter x1, waiting for transfers between devices, shards(): lax.psum_scatter(jnp.concatenate([local_product(tokens, w_gate), local_pr...  56.9 us
    all_gather x1, waiting for transfers between devices, shards(): gathered = lax.all_gather(paired, 'inp', axis=0, tiled=True)  56.9 us
    reduce_scatter x1, waiting for transfers between devices, shards(): lax.psum_scatter(input_terms, 'out', scatter_dimension=1, tiled=True)  25.9 us
    dot_general x2, matrix products, contract_cols(): lax.dot_general(left, right, (((1,), (1,)), ((), ())), preferred_element_...  19.9 us
    dot_general x2, matrix products, local_product(): return jnp.dot(left, right, preferred_element_type=jnp.float32)  11.6 us
    dot_general x1, matrix products, contract_rows(): lax.dot_general(left, right, (((0,), (0,)), ((), ())), preferred_element_...  10 us
  transfers between devices with their start and end apart: 5, of which 4 were waited for; matrix products, arithmetic and copies ran while one was open for 1% of the time, Pallas kernels for 0%

profile of v1, /device:TPU:0, one launch (start us, length us, event | category | flops | bytes accessed | tf_op | source)
XLA Modules:
  0.0 283.4 jit_solution(11789034245816707913)
XLA Ops:
  8.0 0.0 reduce-scatter.3.cloned.1.call-start
  8.1 8.6 %convolution_convert_fusion.1 = bf16[192,3584]{1,0:T(8,128)(2,1)S(1)} fusion(bf16[192,2048]{1,0:T(8,128)(2,1)} %param.4, bf16[2048,3584]{1,0:T(8,128)(2,1)} %param.6), kind=kOutput, calls=%fused_computation.2 | convolution fusion | flops 2819260416 | bytes 16842752 | tf_op jit(solution)/shard_map/dot_general | solution.py:10
  16.7 1.2 copy-done.2
  17.9 3.0 %convolution_convert_fusion = bf16[192,3584]{1,0:T(8,128)(2,1)S(1)} fusion(bf16[192,2048]{1,0:T(8,128)(2,1)S(1)} %copy-done.1, bf16[2048,3584]{1,0:T(8,128)(2,1)S(1)} %copy-done.2), kind=kOutput, calls=%fused_computation.1 | convolution fusion | flops 2819260416 | bytes 16842752 | tf_op jit(solution)/shard_map/dot_general | solution.py:10
  20.9 1.9 pad_maximum_fusion
  22.8 0.0 all-gather.4.cloned.1.call-start
  22.8 56.9 %reduce-scatter.3.cloned.1.call-done = bf16[48,7168]{1,0:T(8,128)(2,1)} async-done(((bf16[192,7168]{1,0:T(8,128)(2,1)}), bf16[48,7168]{1,0:T(8,128)(2,1)}) %reduce-scatter.3.cloned.1.call-update) | async-done | bytes 688144 | tf_op jit(solution)/shard_map/reduce_scatter | solution.py:30
  79.8 1.2 convert_element_type.20
  81.0 1.3 fusion.6
  82.3 0.9 pad_maximum_fusion.1
  83.2 0.0 all-gather.4.cloned.1.call-update
  83.2 0.0 reduce-scatter.5.cloned.1.call-start
  83.2 56.9 %all-gather.4.cloned.1.call-done = bf16[192,7168]{1,0:T(8,128)(2,1)} async-done(((bf16[48,7168]{1,0:T(8,128)(2,1)}), bf16[192,7168]{1,0:T(8,128)(2,1)}) %all-gather.4.cloned.1.call-update) | async-done | bytes 2752528 | tf_op jit(solution)/shard_map/all_gather | solution.py:49
  140.1 8.6 %fusion.1 = f32[192,2048]{1,0:T(8,128)S(1)} fusion(bf16[2048,3584]{1,0:T(8,128)(2,1)} %param.6, bf16[192,7168]{1,0:T(8,128)(2,1)} %all-gather.4.cloned.1.call-done), kind=kOutput, calls=%fused_computation.6 | convolution fusion | flops 2818572288 | bytes 17629184 | tf_op jit(solution)/shard_map/dot_general | solution.py:20
  148.7 11.2 %convolution_add_fusion = f32[192,2048]{1,0:T(8,128)} fusion(f32[192,2048]{1,0:T(8,128)S(1)} %fusion.1, bf16[2048,3584]{1,0:T(8,128)(2,1)} %param.7, bf16[192,7168]{1,0:T(8,128)(2,1)S(1)} %copy-done), kind=kOutput, calls=%fused_computation.4 | convolution fusion | flops 2818965504 | bytes 19202048 | tf_op jit(solution)/shard_map/dot_general | solution.py:20
  160.0 0.0 all-gather.6.cloned.1.call-start
  160.0 0.5 all-gather.6.cloned.1.call-update
  160.6 0.2 all-gather.8.cloned.1.call-start
  160.8 0.4 all-gather.8.cloned.1.call-update
  161.2 25.9 %reduce-scatter.5.cloned.1.call-done = f32[192,512]{1,0:T(8,128)} async-done(((f32[192,2048]{1,0:T(8,128)}), f32[192,512]{1,0:T(8,128)}) %reduce-scatter.5.cloned.1.call-update) | async-done | bytes 393232 | tf_op jit(solution)/shard_map/reduce_scatter | solution.py:53
  187.1 1.7 convert_element_type.23
  188.8 72.0 %all-gather.8.cloned.1.call-done = bf16[384,7168]{1,0:T(8,128)(2,1)} async-done(((bf16[192,7168]{1,0:T(8,128)(2,1)}), bf16[384,7168]{1,0:T(8,128)(2,1)}) %all-gather.8.cloned.1.call-update) | async-done | bytes 5505040 | tf_op jit(solution)/shard_map/all_gather | solution.py:62
  260.7 10.0 %multiply_convert_fusion = bf16[1024,7168]{1,0:T(8,128)(2,1)S(1)} fusion(bf16[384,7168]{1,0:T(8,128)(2,1)} %all-gather.8.cloned.1.call-done, bf16[384,2048]{1,0:T(8,128)(2,1)} %all-gather.6.cloned.1.call-done, s32[]{:T(128)S(6)} %select_n.7), kind=kOutput, calls=%fused_computation | convolution fusion | flops 5651824640 | bytes 20971524 | tf_op jit(solution)/shard_map/dot_general | solution.py:14
  270.8 5.5 %fusion.10 = (bf16[1024,3584]{1,0:T(8,128)(2,1)}, bf16[1024,3584]{1,0:T(8,128)(2,1)}) fusion(bf16[1024,7168]{1,0:T(8,128)(2,1)S(1)} %multiply_convert_fusion), kind=kLoop, calls=%fused_computation.19 | loop fusion | bytes 29360128 | tf_op jit(solution)/shard_map/slice | solution.py:64
  (8 shorter events, 0.0 us)
Async XLA Ops:
  8.0 8.6 %copy-start.1 = (bf16[192,2048]{1,0:T(8,128)(2,1)S(1)}, bf16[192,2048]{1,0:T(8,128)(2,1)}, u32[]{:S(2)}) copy-start(bf16[192,2048]{1,0:T(8,128)(2,1)} %param.4) | copy-start | bytes 2359300
  8.0 71.8 %reduce-scatter.3.cloned.1.call-start = ((), (), s32[]{:S(2)}) async-start(), calls=%async_computation.2 | async-start | bytes 3440640 | tf_op jit(solution)/shard_map/reduce_scatter | solution.py:30
  8.1 9.8 %copy-start.2 = (bf16[2048,3584]{1,0:T(8,128)(2,1)S(1)}, bf16[2048,3584]{1,0:T(8,128)(2,1)}, u32[]{:S(2)}) copy-start(bf16[2048,3584]{1,0:T(8,128)(2,1)} %param.7) | copy-start | bytes 44040196
  22.8 117.3 %all-gather.4.cloned.1.call-start = ((), (), s32[]{:S(2)}) async-start(), calls=%async_computation.3 | async-start | bytes 3440640 | tf_op jit(solution)/shard_map/all_gather | solution.py:49
  83.2 103.9 %reduce-scatter.5.cloned.1.call-start = ((), (), s32[]{:S(2)}) async-start(), calls=%async_computation.4 | async-start | bytes 1966080 | tf_op jit(solution)/shard_map/reduce_scatter | solution.py:53
  140.1 8.6 %copy-start = (bf16[192,7168]{1,0:T(8,128)(2,1)S(1)}, bf16[192,7168]{1,0:T(8,128)(2,1)}, u32[]{:S(2)}) copy-start(bf16[192,7168]{1,0:T(8,128)(2,1)} %all-gather.4.cloned.1.call-done) | copy-start | bytes 8257540
  160.0 28.8 %all-gather.6.cloned.1.call-start = ((), (), s32[]{:S(2)}) async-start(), calls=%async_computation.5 | async-start | bytes 2359296 | tf_op jit(solution)/shard_map/all_gather | solution.py:57
  160.6 100.2 %all-gather.8.cloned.1.call-start = ((), (), s32[]{:S(2)}) async-start(), calls=%async_computation.6 | async-start | bytes 8257536 | tf_op jit(solution)/shard_map/all_gather | solution.py:62
Sparse Core Ops, SparseCore 0:
  22.9 56.8 reduce-scatter.2
  83.3 56.7 all-gather.3
  160.1 26.9 reduce-scatter.4
Sparse Core Ops, SparseCore 1:
  162.1 25.7 all-gather.5
  189.4 71.3 all-gather.7

commit v2 on v0

v2 whole, which is shorter than its diff:
```python
import math

import jax
import jax.numpy as jnp
from jax import lax
from jax.sharding import PartitionSpec as P

CHUNKS = 2


def local_product(left, right):
    return jnp.dot(left, right, preferred_element_type=jnp.float32)


def contract_rows(left, right):
    return lax.dot_general(
        left, right, (((0,), (0,)), ((), ())), preferred_element_type=jnp.float32
    )


def contract_cols(left, right):
    return lax.dot_general(
        left, right, (((1,), (1,)), ((), ())), preferred_element_type=jnp.float32
    )


def activation_grads(gate_value, up_value, cotangent):
    sigmoid_gate = jax.nn.sigmoid(gate_value)
    grad_gate = cotangent * up_value * sigmoid_gate * (1.0 + gate_value * (1.0 - sigmoid_gate))
    grad_upper = cotangent * gate_value * sigmoid_gate
    return jnp.concatenate(
        [grad_gate.astype(jnp.bfloat16), grad_upper.astype(jnp.bfloat16)], axis=1
    )


def shards(tokens, grad_hidden, w_gate, w_up):
    token_count = tokens.shape[0]
    own_rows = token_count // lax.axis_size("inp")
    chunk = w_gate.shape[1] // CHUNKS
    dep_count = lax.axis_size("dep")
    dep_index = lax.axis_index("dep")
    factor = 1.0 / math.sqrt(token_count * dep_count)
    offset = lax.axis_index("inp") * own_rows
    cotangent = lax.dynamic_slice_in_dim(grad_hidden, offset, own_rows, 0).astype(jnp.float32)

    own_features = tokens.shape[1] // dep_count
    every_token = lax.all_gather(tokens, "dep", axis=0, tiled=True)
    own_tokens = lax.dynamic_slice_in_dim(every_token, dep_index * own_features, own_features, 1)

    every_grad = []
    for step in range(CHUNKS):
        columns = slice(step * chunk, (step + 1) * chunk)
        partial = jnp.concatenate(
            [local_product(tokens, w_gate[:, columns]), local_product(tokens, w_up[:, columns])],
            axis=1,
        ).astype(jnp.bfloat16)
        summed = lax.psum_scatter(partial, "inp", scatter_dimension=0, tiled=True)
        summed = summed.astype(jnp.float32)
        paired = activation_grads(summed[:, :chunk], summed[:, chunk:], cotangent[:, columns])
        every_grad.append(lax.all_gather(paired, ("dep", "inp"), axis=0, tiled=True))

    input_terms = 0.0
    for step, both in enumerate(every_grad):
        columns = slice(step * chunk, (step + 1) * chunk)
        own = lax.dynamic_slice_in_dim(both, dep_index * token_count, token_count, 0)
        input_terms += contract_cols(own[:, :chunk], w_gate[:, columns])
        input_terms += contract_cols(own[:, chunk:], w_up[:, columns])
    grad_input = lax.psum_scatter(
        input_terms.astype(jnp.bfloat16), "out", scatter_dimension=1, tiled=True
    )
    every_gate = jnp.concatenate([both[:, :chunk] for both in every_grad], axis=1)
    every_upper = jnp.concatenate([both[:, chunk:] for both in every_grad], axis=1)
    return (
        grad_input,
        (contract_rows(own_tokens, every_gate) * factor).astype(jnp.bfloat16),
        (contract_rows(own_tokens, every_upper) * factor).astype(jnp.bfloat16),
    )


def solution(mesh):
    return jax.shard_map(
        shards,
        mesh=mesh,
        in_specs=(P("dep", "inp"), P("dep", "out"), P("inp", "out"), P("inp", "out")),
        out_specs=(P("dep", ("inp", "out")), P(("inp", "dep"), "out"), P(("inp", "dep"), "out")),
        check_vma=False,
    )
```

time: 596 us -> 262 us (0.44)
  waiting for transfers between devices: 489 us -> 174 us
  local copies, waits for them, and re-layouts: 23.6 us -> 4.05 us
  matrix products: 44.7 us -> 61.4 us
  other arithmetic: 23.8 us -> 7.27 us
    reduce_scatter x4 -> x3, waiting for transfers between devices: 431 us -> 67.6 us  [the longest x2 56.4 us: shards(): summed = lax.psum_scatter(partial, 'inp', scatter_dimension=0, tiled=True)]
    all_gather x1 -> x3, waiting for transfers between devices: 57.6 us -> 106 us  [the longest x2 96.3 us: shards(): lax.all_gather(paired, ('dep', 'inp'), axis=0, tiled=True)]
    unnamed x8 -> x16, local copies, waits for them, and re-layouts: 23.6 us -> 1.08 us
    convert_element_type x4, other arithmetic: 20 us -> 3.43 us  [the longest x2 2.05 us: shards(): summed = summed.astype(jnp.float32)]
    dot_general x2 -> x4, matrix products: 10 us -> 19.1 us  [local_product(): return jnp.dot(left, right, preferred_element_type=jnp.float32)]
    dot_general x2 -> x4, matrix products: 19.8 us -> 27.3 us  [contract_cols(): lax.dot_general(left, right, (((1,), (1,)), ((), ())), preferred_element_...]
  transfers between devices with their start and end apart: 5 -> 6, of which waited for: 5 -> 6; matrix products, arithmetic and copies ran while one was open for 6% -> 22% of each run, Pallas kernels for 0% -> 0%
where the time goes in v2:
time: 262 us
  waiting for transfers between devices  174 us (66%)
  matrix products  61.4 us (23%)
  between operations  14.2 us (5%)
  other arithmetic  7.27 us (3%)
  local copies, waits for them, and re-layouts  4.05 us (2%)
    all_gather x2, waiting for transfers between devices, shards(): lax.all_gather(paired, ('dep', 'inp'), axis=0, tiled=True)  96.3 us
    reduce_scatter x2, waiting for transfers between devices, shards(): summed = lax.psum_scatter(partial, 'inp', scatter_dimension=0, tiled=True)  56.4 us
    dot_general x4, matrix products, contract_cols(): lax.dot_general(left, right, (((1,), (1,)), ((), ())), preferred_element_...  27.3 us
    dot_general x4, matrix products, local_product(): return jnp.dot(left, right, preferred_element_type=jnp.float32)  19.1 us
    dot_general x2, matrix products, contract_rows(): lax.dot_general(left, right, (((0,), (0,)), ((), ())), preferred_element_...  15 us
    reduce_scatter x1, waiting for transfers between devices, shards(): lax.psum_scatter(input_terms.astype(jnp.bfloat16), 'out', scatter_dimensi...  11.2 us
    all_gather x1, waiting for transfers between devices, shards(): every_token = lax.all_gather(tokens, 'dep', axis=0, tiled=True)  9.93 us
  transfers between devices with their start and end apart: 6, of which 6 were waited for; matrix products, arithmetic and copies ran while one was open for 22% of the time, Pallas kernels for 0%

profile of v2, /device:TPU:0, one launch (start us, length us, event | category | flops | bytes accessed | tf_op | source)
XLA Modules:
  0.0 261.9 jit_solution(13483352866322492797)
XLA Ops:
  7.2 5.0 %fusion.40 = bf16[192,1792]{1,0:T(8,128)(2,1)S(1)} fusion(bf16[192,2048]{1,0:T(8,128)(2,1)} %param.4, bf16[2048,3584]{1,0:T(8,128)(2,1)} %param.6), kind=kOutput, calls=%fused_computation.30 | convolution fusion | flops 1409630208 | bytes 8814592 | tf_op jit(solution)/shard_map/dot_general | solution.py:12
  12.2 4.7 %fusion.43 = bf16[192,1792]{1,0:T(8,128)(2,1)S(1)} fusion(bf16[192,2048]{1,0:T(8,128)(2,1)S(1)} %copy-done.4, bf16[2048,3584]{1,0:T(8,128)(2,1)} %param.7), kind=kOutput, calls=%fused_computation.31 | convolution fusion | flops 1409630208 | bytes 8814592 | tf_op jit(solution)/shard_map/dot_general | solution.py:12
  16.9 1.2 pad_maximum_fusion.1
  18.2 4.7 %fusion.34 = bf16[192,1792]{1,0:T(8,128)(2,1)S(1)} fusion(bf16[192,2048]{1,0:T(8,128)(2,1)S(1)} %copy-done.4, bf16[2048,3584]{1,0:T(8,128)(2,1)} %param.6), kind=kOutput, calls=%fused_computation.28 | convolution fusion | flops 1409630208 | bytes 8814592 | tf_op jit(solution)/shard_map/dot_general | solution.py:12
  22.8 4.7 %fusion.37 = bf16[192,1792]{1,0:T(8,128)(2,1)S(1)} fusion(bf16[192,2048]{1,0:T(8,128)(2,1)S(1)} %copy-done.4, bf16[2048,3584]{1,0:T(8,128)(2,1)} %param.7), kind=kOutput, calls=%fused_computation.29 | convolution fusion | flops 1409630208 | bytes 8814592 | tf_op jit(solution)/shard_map/dot_general | solution.py:12
  27.6 1.2 pad_maximum_fusion
  28.8 1.0 dynamic-slice_convert_fusion
  29.9 23.3 %reduce-scatter.6.cloned.1.call-done = bf16[48,3584]{1,0:T(8,128)(2,1)} async-done(((bf16[192,3584]{1,0:T(8,128)(2,1)}), bf16[48,3584]{1,0:T(8,128)(2,1)}) %reduce-scatter.6.cloned.1.call-update) | async-done | bytes 344080 | tf_op jit(solution)/shard_map/reduce_scatter | solution.py:57
  53.2 1.0 convert_element_type.36
  54.2 33.0 %reduce-scatter.4.cloned.1.call-done = bf16[48,3584]{1,0:T(8,128)(2,1)} async-done(((bf16[192,3584]{1,0:T(8,128)(2,1)}), bf16[48,3584]{1,0:T(8,128)(2,1)}) %reduce-scatter.4.cloned.1.call-update) | async-done | bytes 344080 | tf_op jit(solution)/shard_map/reduce_scatter | solution.py:57
  87.3 1.0 convert_element_type.33
  91.1 53.8 %all-gather.6.cloned.1.call-done = bf16[384,3584]{1,0:T(8,128)(2,1)} async-done(((bf16[48,3584]{1,0:T(8,128)(2,1)}), bf16[384,3584]{1,0:T(8,128)(2,1)}) %all-gather.6.cloned.1.call-update) | async-done | bytes 2752528 | tf_op jit(solution)/shard_map/all_gather | solution.py:60
  144.9 7.1 %fusion.4 = f32[192,2048]{1,0:T(8,128)} fusion(bf16[2048,3584]{1,0:T(8,128)(2,1)} %param.6, bf16[384,3584]{1,0:T(8,128)(2,1)} %all-gather.6.cloned.1.call-done, s32[]{:T(128)S(6)} %select_n.11), kind=kOutput, calls=%fused_computation.6 | convolution fusion | flops 1409286144 | bytes 9601028 | tf_op jit(solution)/shard_map/dot_general | solution.py:22
  152.0 7.0 %fusion = f32[192,2048]{1,0:T(8,128)} fusion(bf16[2048,3584]{1,0:T(8,128)(2,1)} %param.7, bf16[384,3584]{1,0:T(8,128)(2,1)S(1)} %copy-done, s32[]{:T(128)S(6)} %select_n.11, s32[]{:T(128)S(6)} %add.47), kind=kOutput, calls=%fused_computation.2 | convolution fusion | flops 1409286144 | bytes 9601032 | tf_op jit(solution)/shard_map/dot_general | solution.py:22
  159.0 42.5 %all-gather.4.cloned.1.call-done = bf16[384,3584]{1,0:T(8,128)(2,1)} async-done(((bf16[48,3584]{1,0:T(8,128)(2,1)}), bf16[384,3584]{1,0:T(8,128)(2,1)}) %all-gather.4.cloned.1.call-update) | async-done | bytes 2752528 | tf_op jit(solution)/shard_map/all_gather | solution.py:60
  201.5 6.0 %fusion.8 = f32[192,2048]{1,0:T(8,128)S(1)} fusion(bf16[2048,3584]{1,0:T(8,128)(2,1)} %param.7, bf16[384,3584]{1,0:T(8,128)(2,1)} %all-gather.4.cloned.1.call-done, s32[]{:T(128)S(6)} %select_n.11, s32[]{:T(128)S(6)} %add.47), kind=kOutput, calls=%fused_computation.10 | convolution fusion | flops 1409286144 | bytes 9601032 | tf_op jit(solution)/shard_map/dot_general | solution.py:22
  207.5 7.3 %fusion.31 = bf16[192,2048]{1,0:T(8,128)(2,1)} fusion(f32[192,2048]{1,0:T(8,128)S(1)} %copy-done.7, f32[192,2048]{1,0:T(8,128)S(1)} %copy-done.6, f32[192,2048]{1,0:T(8,128)S(1)} %fusion.8, bf16[2048,3584]{1,0:T(8,128)(2,1)} %param.6, bf16[384,3584]{1,0:T(8,128)(2,1)} %all-gather.4.cloned.1.call-done, s32[]{:T(128)S(6)} %select_n.11), kind=kOutput, calls=%fused_computation.27 | convolution fusion | flops 1410859008 | bytes 13533188 | tf_op jit(solution)/shard_map/dot_general | solution.py:22
  214.8 1.7 fusion.65
  216.5 1.1 copy-done.1
  217.6 1.3 fusion.64
  218.8 9.9 %all-gather.8.cloned.1.call-done = bf16[384,2048]{1,0:T(8,128)(2,1)} async-done(((bf16[192,2048]{1,0:T(8,128)(2,1)}), bf16[384,2048]{1,0:T(8,128)(2,1)}) %all-gather.8.cloned.1.call-update) | async-done | bytes 1572880 | tf_op jit(solution)/shard_map/all_gather | solution.py:47
  228.8 8.8 %multiply_convert_fusion = bf16[1024,3584]{1,0:T(8,128)(2,1)} fusion(bf16[384,1792]{1,0:T(8,128)(2,1)S(1)} %copy-done.3, bf16[384,1792]{1,0:T(8,128)(2,1)} %get-tuple-element.3, bf16[384,2048]{1,0:T(8,128)(2,1)} %all-gather.8.cloned.1.call-done, s32[]{:T(128)S(6)} %select_n.12), kind=kOutput, calls=%fused_computation | convolution fusion | flops 2831417344 | bytes 10878980 | tf_op jit(solution)/shard_map/dot_general | solution.py:16
  237.6 6.2 %multiply_convert_fusion.1 = bf16[1024,3584]{1,0:T(8,128)(2,1)} fusion(bf16[384,1792]{1,0:T(8,128)(2,1)S(1)} %copy-done.2, bf16[384,1792]{1,0:T(8,128)(2,1)S(1)} %get-tuple-element.4, bf16[384,2048]{1,0:T(8,128)(2,1)S(1)} %copy-done.5, s32[]{:T(128)S(6)} %select_n.12), kind=kOutput, calls=%fused_computation.1 | convolution fusion | flops 2831417344 | bytes 10878980 | tf_op jit(solution)/shard_map/dot_general | solution.py:16
  243.8 11.2 %reduce-scatter.8.cloned.1.call-done = bf16[192,512]{1,0:T(8,128)(2,1)} async-done(((bf16[192,2048]{1,0:T(8,128)(2,1)}), bf16[192,512]{1,0:T(8,128)(2,1)}) %reduce-scatter.8.cloned.1.call-update) | async-done | bytes 196624 | tf_op jit(solution)/shard_map/reduce_scatter | solution.py:68
  (30 shorter events, 2.9 us)
Async XLA Ops:
  7.2 5.1 %copy-start.4 = (bf16[192,2048]{1,0:T(8,128)(2,1)S(1)}, bf16[192,2048]{1,0:T(8,128)(2,1)}, u32[]{:S(2)}) copy-start(bf16[192,2048]{1,0:T(8,128)(2,1)} %param.4) | copy-start | bytes 2359300
  7.2 46.0 %reduce-scatter.6.cloned.1.call-start = ((), (), s32[]{:S(2)}) async-start(), calls=%async_computation.5 | async-start | bytes 1720320 | tf_op jit(solution)/shard_map/reduce_scatter | solution.py:57
  18.1 69.2 %reduce-scatter.4.cloned.1.call-start = ((), (), s32[]{:S(2)}) async-start(), calls=%async_computation.3 | async-start | bytes 1720320 | tf_op jit(solution)/shard_map/reduce_scatter | solution.py:57
  28.8 116.1 %all-gather.6.cloned.1.call-start = ((), (), s32[]{:S(2)}) async-start(), calls=%async_computation.6 | async-start | bytes 3096576 | tf_op jit(solution)/shard_map/all_gather | solution.py:60
  89.4 112.1 %all-gather.4.cloned.1.call-start = ((), (), s32[]{:S(2)}) async-start(), calls=%async_computation.4 | async-start | bytes 3096576 | tf_op jit(solution)/shard_map/all_gather | solution.py:60
  90.3 138.5 %all-gather.8.cloned.1.call-start = ((), (), s32[]{:S(2)}) async-start(), calls=%async_computation.8 | async-start | bytes 2359296 | tf_op jit(solution)/shard_map/all_gather | solution.py:47
  90.9 164.2 %reduce-scatter.8.cloned.1.call-start = ((), (), s32[]{:S(2)}) async-start(), calls=%async_computation.7 | async-start | bytes 983040 | tf_op jit(solution)/shard_map/reduce_scatter | solution.py:68
  144.9 7.1 %copy-start = (bf16[384,3584]{1,0:T(8,128)(2,1)S(1)}, bf16[384,3584]{1,0:T(8,128)(2,1)}, u32[]{:S(2)}) copy-start(bf16[384,3584]{1,0:T(8,128)(2,1)} %all-gather.6.cloned.1.call-done) | copy-start | bytes 8257540
  201.5 6.0 %copy-start.6 = (f32[192,2048]{1,0:T(8,128)S(1)}, f32[192,2048]{1,0:T(8,128)}, u32[]{:S(2)}) copy-start(f32[192,2048]{1,0:T(8,128)} %fusion.4) | copy-start | bytes 4718596
  201.5 6.0 %copy-start.7 = (f32[192,2048]{1,0:T(8,128)S(1)}, f32[192,2048]{1,0:T(8,128)}, u32[]{:S(2)}) copy-start(f32[192,2048]{1,0:T(8,128)} %fusion) | copy-start | bytes 4718596
  214.8 2.8 %copy-start.1 = (bf16[384,3584]{1,0:T(8,128)(2,1)S(1)}, bf16[384,3584]{1,0:T(8,128)(2,1)}, u32[]{:S(2)}) copy-start(bf16[384,3584]{1,0:T(8,128)(2,1)} %all-gather.4.cloned.1.call-done) | copy-start | bytes 8257540
  217.6 11.2 %copy-start.3 = (bf16[384,1792]{1,0:T(8,128)(2,1)S(1)}, bf16[384,1792]{1,0:T(8,128)(2,1)}, u32[]{:S(2)}) copy-start(bf16[384,1792]{1,0:T(8,128)(2,1)} %get-tuple-element.5) | copy-start | bytes 4128772
  228.8 8.8 %copy-start.2 = (bf16[384,1792]{1,0:T(8,128)(2,1)S(1)}, bf16[384,1792]{1,0:T(8,128)(2,1)}, u32[]{:S(2)}) copy-start(bf16[384,1792]{1,0:T(8,128)(2,1)} %get-tuple-element.6) | copy-start | bytes 4128772
  228.8 8.8 %copy-start.5 = (bf16[384,2048]{1,0:T(8,128)(2,1)S(1)}, bf16[384,2048]{1,0:T(8,128)(2,1)}, u32[]{:S(2)}) copy-start(bf16[384,2048]{1,0:T(8,128)(2,1)} %all-gather.8.cloned.1.call-done) | copy-start | bytes 4718596
Sparse Core Ops, SparseCore 0:
  18.2 34.9 reduce-scatter.5
  56.2 31.0 reduce-scatter.3
  90.0 54.8 all-gather.5
  146.8 54.6 all-gather.3
  202.9 25.8 all-gather.7
  231.7 23.2 reduce-scatter.7

commit v3 on v2

--- a/solution.py
+++ b/solution.py
@@ -44,8 +44,19 @@
     cotangent = lax.dynamic_slice_in_dim(grad_hidden, offset, own_rows, 0).astype(jnp.float32)
 
     own_features = tokens.shape[1] // dep_count
-    every_token = lax.all_gather(tokens, "dep", axis=0, tiled=True)
-    own_tokens = lax.dynamic_slice_in_dim(every_token, dep_index * own_features, own_features, 1)
+
+    def token_columns(owner):
+        return lax.dynamic_slice_in_dim(tokens, owner * own_features, own_features, 1)
+
+    def shifted(array, shift):
+        return lax.ppermute(array, "dep", [(i, (i + shift) % dep_count) for i in range(dep_count)])
+
+    shifts = range(1, dep_count)
+    every_token = jnp.concatenate(
+        [token_columns(dep_index)]
+        + [shifted(token_columns((dep_index + shift) % dep_count), shift) for shift in shifts],
+        axis=0,
+    )
 
     every_grad = []
     for step in range(CHUNKS):
@@ -57,23 +68,27 @@
         summed = lax.psum_scatter(partial, "inp", scatter_dimension=0, tiled=True)
         summed = summed.astype(jnp.float32)
         paired = activation_grads(summed[:, :chunk], summed[:, chunk:], cotangent[:, columns])
-        every_grad.append(lax.all_gather(paired, ("dep", "inp"), axis=0, tiled=True))
+        every_grad.append(lax.all_gather(paired, "inp", axis=0, tiled=True))
 
     input_terms = 0.0
-    for step, both in enumerate(every_grad):
+    for step, own in enumerate(every_grad):
         columns = slice(step * chunk, (step + 1) * chunk)
-        own = lax.dynamic_slice_in_dim(both, dep_index * token_count, token_count, 0)
         input_terms += contract_cols(own[:, :chunk], w_gate[:, columns])
         input_terms += contract_cols(own[:, chunk:], w_up[:, columns])
     grad_input = lax.psum_scatter(
         input_terms.astype(jnp.bfloat16), "out", scatter_dimension=1, tiled=True
     )
-    every_gate = jnp.concatenate([both[:, :chunk] for both in every_grad], axis=1)
-    every_upper = jnp.concatenate([both[:, chunk:] for both in every_grad], axis=1)
+    by_owner = [every_grad] + [[shifted(own, shift) for own in every_grad] for shift in shifts]
+    every_gate = jnp.concatenate(
+        [jnp.concatenate([both[:, :chunk] for both in chunks], axis=1) for chunks in by_owner], axis=0
+    )
+    every_upper = jnp.concatenate(
+        [jnp.concatenate([both[:, chunk:] for both in chunks], axis=1) for chunks in by_owner], axis=0
+    )
     return (
         grad_input,
-        (contract_rows(own_tokens, every_gate) * factor).astype(jnp.bfloat16),
-        (contract_rows(own_tokens, every_upper) * factor).astype(jnp.bfloat16),
+        (contract_rows(every_token, every_gate) * factor).astype(jnp.bfloat16),
+        (contract_rows(every_token, every_upper) * factor).astype(jnp.bfloat16),
     )
 
 

time: 262 us -> 238 us (0.908)
  waiting for transfers between devices: 174 us -> 134 us
  matrix products: 61.4 us -> 76.2 us
  starting transfers between devices: 0.42 us -> 4.93 us
    all_gather x3 -> x2, waiting for transfers between devices: 106 us -> 49.1 us  [shards(): every_grad.append(lax.all_gather(paired, 'inp', axis=0, tiled=True))]
    ppermute x0 -> x3, waiting for transfers between devices: none -> 28.2 us  [shifted(): lax.ppermute(array, 'dep', [(i, (i + shift) % dep_count) for i in range(d...]
    dot_general x2, matrix products: 15 us -> 31 us  [contract_rows(): lax.dot_general(left, right, (((0,), (0,)), ((), ())), preferred_element_...]
    reduce_scatter x1, waiting for transfers between devices: 11.2 us -> 0.01 us  [shards(): lax.psum_scatter(input_terms.astype(jnp.bfloat16), 'out', scatter_dimensi...]
    ppermute x0 -> x3, starting transfers between devices: none -> 4.54 us  [shifted(): lax.ppermute(array, 'dep', [(i, (i + shift) % dep_count) for i in range(d...]
  transfers between devices with their start and end apart: 6 -> 8, of which waited for: 6 -> 5; matrix products, arithmetic and copies ran while one was open for 22% -> 30% of each run, Pallas kernels for 0% -> 0%
where the time goes in v3:
time: 238 us
  waiting for transfers between devices  134 us (56%)
  matrix products  76.2 us (32%)
  between operations  13.9 us (6%)
  other arithmetic  7.3 us (3%)
  starting transfers between devices  4.93 us (2%)
    reduce_scatter x2, waiting for transfers between devices, shards(): summed = lax.psum_scatter(partial, 'inp', scatter_dimension=0, tiled=True)  56.4 us
    all_gather x2, waiting for transfers between devices, shards(): every_grad.append(lax.all_gather(paired, 'inp', axis=0, tiled=True))  49.1 us
    dot_general x2, matrix products, contract_rows(): lax.dot_general(left, right, (((0,), (0,)), ((), ())), preferred_element_...  31 us
    ppermute x3, waiting for transfers between devices, shifted(): lax.ppermute(array, 'dep', [(i, (i + shift) % dep_count) for i in range(d...  28.2 us
    dot_general x4, matrix products, contract_cols(): lax.dot_general(left, right, (((1,), (1,)), ((), ())), preferred_element_...  26.2 us
    dot_general x4, matrix products, local_product(): return jnp.dot(left, right, preferred_element_type=jnp.float32)  19.1 us
  transfers between devices with their start and end apart: 8, of which 5 were waited for; matrix products, arithmetic and copies ran while one was open for 30% of the time, Pallas kernels for 0%

profile of v3, /device:TPU:0, one launch (start us, length us, event | category | flops | bytes accessed | tf_op | source)
XLA Modules:
  0.0 237.9 jit_solution(10091129680299425335)
XLA Ops:
  7.2 5.0 %fusion.48 = bf16[192,1792]{1,0:T(8,128)(2,1)S(1)} fusion(bf16[192,2048]{1,0:T(8,128)(2,1)} %param.4, bf16[2048,3584]{1,0:T(8,128)(2,1)} %param.6), kind=kOutput, calls=%fused_computation.38 | convolution fusion | flops 1409630208 | bytes 8814592 | tf_op jit(solution)/shard_map/dot_general | solution.py:12
  12.2 4.7 %fusion.51 = bf16[192,1792]{1,0:T(8,128)(2,1)S(1)} fusion(bf16[192,2048]{1,0:T(8,128)(2,1)S(1)} %copy-done.2, bf16[2048,3584]{1,0:T(8,128)(2,1)} %param.7), kind=kOutput, calls=%fused_computation.39 | convolution fusion | flops 1409630208 | bytes 8814592 | tf_op jit(solution)/shard_map/dot_general | solution.py:12
  16.9 1.2 pad_maximum_fusion.1
  18.2 4.7 %fusion.42 = bf16[192,1792]{1,0:T(8,128)(2,1)S(1)} fusion(bf16[192,2048]{1,0:T(8,128)(2,1)S(1)} %copy-done.2, bf16[2048,3584]{1,0:T(8,128)(2,1)} %param.6), kind=kOutput, calls=%fused_computation.36 | convolution fusion | flops 1409630208 | bytes 8814592 | tf_op jit(solution)/shard_map/dot_general | solution.py:12
  22.8 4.7 %fusion.45 = bf16[192,1792]{1,0:T(8,128)(2,1)S(1)} fusion(bf16[192,2048]{1,0:T(8,128)(2,1)S(1)} %copy-done.2, bf16[2048,3584]{1,0:T(8,128)(2,1)} %param.7), kind=kOutput, calls=%fused_computation.37 | convolution fusion | flops 1409630208 | bytes 8814592 | tf_op jit(solution)/shard_map/dot_general | solution.py:12
  27.6 1.2 pad_maximum_fusion
  28.8 1.0 dynamic-slice_convert_fusion
  29.9 23.3 %reduce-scatter.6.cloned.1.call-done = bf16[48,3584]{1,0:T(8,128)(2,1)} async-done(((bf16[192,3584]{1,0:T(8,128)(2,1)}), bf16[48,3584]{1,0:T(8,128)(2,1)}) %reduce-scatter.6.cloned.1.call-update) | async-done | bytes 344080 | tf_op jit(solution)/shard_map/reduce_scatter | solution.py:68
  53.2 1.0 convert_element_type.36
  54.2 33.0 %reduce-scatter.4.cloned.1.call-done = bf16[48,3584]{1,0:T(8,128)(2,1)} async-done(((bf16[192,3584]{1,0:T(8,128)(2,1)}), bf16[48,3584]{1,0:T(8,128)(2,1)}) %reduce-scatter.4.cloned.1.call-update) | async-done | bytes 344080 | tf_op jit(solution)/shard_map/reduce_scatter | solution.py:68
  87.3 1.0 convert_element_type.33
  90.6 1.5 collective-permute-start
  92.2 30.1 %all-gather.5.cloned.1.call-done = bf16[192,3584]{1,0:T(8,128)(2,1)} async-done(((bf16[48,3584]{1,0:T(8,128)(2,1)}), bf16[192,3584]{1,0:T(8,128)(2,1)}) %all-gather.5.cloned.1.call-update) | async-done | bytes 1376272 | tf_op jit(solution)/shard_map/all_gather | solution.py:71
  122.3 1.5 collective-permute-start.2
  123.8 7.0 %fusion = f32[192,2048]{1,0:T(8,128)} fusion(bf16[2048,3584]{1,0:T(8,128)(2,1)} %param.7, bf16[192,3584]{1,0:T(8,128)(2,1)} %all-gather.5.cloned.1.call-done), kind=kOutput, calls=%fused_computation.2 | convolution fusion | flops 1409286144 | bytes 9601024 | tf_op jit(solution)/shard_map/dot_general | solution.py:22
  130.7 6.8 %fusion.4 = f32[192,2048]{1,0:T(8,128)} fusion(bf16[2048,3584]{1,0:T(8,128)(2,1)} %param.6, bf16[192,3584]{1,0:T(8,128)(2,1)S(1)} %copy-done), kind=kOutput, calls=%fused_computation.6 | convolution fusion | flops 1409286144 | bytes 9601024 | tf_op jit(solution)/shard_map/dot_general | solution.py:22
  137.5 19.0 %all-gather.3.cloned.1.call-done = bf16[192,3584]{1,0:T(8,128)(2,1)} async-done(((bf16[48,3584]{1,0:T(8,128)(2,1)}), bf16[192,3584]{1,0:T(8,128)(2,1)}) %all-gather.3.cloned.1.call-update) | async-done | bytes 1376272 | tf_op jit(solution)/shard_map/all_gather | solution.py:71
  156.5 6.0 %fusion.8 = f32[192,2048]{1,0:T(8,128)S(1)} fusion(bf16[2048,3584]{1,0:T(8,128)(2,1)} %param.7, bf16[192,3584]{1,0:T(8,128)(2,1)} %all-gather.3.cloned.1.call-done), kind=kOutput, calls=%fused_computation.10 | convolution fusion | flops 1409286144 | bytes 9601024 | tf_op jit(solution)/shard_map/dot_general | solution.py:22
  162.5 6.5 %fusion.39 = bf16[192,2048]{1,0:T(8,128)(2,1)} fusion(f32[192,2048]{1,0:T(8,128)S(1)} %copy-done.3, f32[192,2048]{1,0:T(8,128)S(1)} %copy-done.4, f32[192,2048]{1,0:T(8,128)S(1)} %fusion.8, bf16[2048,3584]{1,0:T(8,128)(2,1)} %param.6, bf16[192,3584]{1,0:T(8,128)(2,1)S(1)} %copy-done.1), kind=kOutput, calls=%fused_computation.35 | convolution fusion | flops 1410859008 | bytes 13533184 | tf_op jit(solution)/shard_map/dot_general | solution.py:22
  169.0 1.5 collective-permute-start.1
  170.7 1.4 fusion.69
  172.1 28.1 %collective-permute-done.1 = bf16[192,3584]{1,0:T(8,128)(2,1)S(1)} collective-permute-done((bf16[192,3584]{1,0:T(8,128)(2,1)S(1)}, bf16[192,3584]{1,0:T(8,128)(2,1)S(1)}, u32[]{:S(2)}, u32[]{:S(2)}) %collective-permute-start.1) | collective-permute-done | bytes 1376288 | tf_op jit(solution)/shard_map/ppermute | solution.py:52
  200.4 15.6 %multiply_convert_fusion = bf16[1024,3584]{1,0:T(8,128)(2,1)} fusion(bf16[192,1792]{1,0:T(8,128)(2,1)S(1)} %get-tuple-element.9, bf16[192,1792]{1,0:T(8,128)(2,1)S(1)} %get-tuple-element.7, bf16[192,1792]{1,0:T(8,128)(2,1)S(1)} %get-tuple-element.5, bf16[192,1792]{1,0:T(8,128)(2,1)S(1)} %get-tuple-element.3, bf16[192,1024]{1,0:T(8,128)(2,1)} %collective-permute-done, ...), kind=kOutput, calls=%fused_computation | convolution fusion | flops 2838495232 | bytes 10878976 | tf_op jit(solution)/shard_map/dot_general | solution.py:16
  216.0 15.4 %multiply_convert_fusion.1 = bf16[1024,3584]{1,0:T(8,128)(2,1)} fusion(bf16[192,1792]{1,0:T(8,128)(2,1)S(1)} %get-tuple-element.10, bf16[192,1792]{1,0:T(8,128)(2,1)S(1)} %get-tuple-element.8, bf16[192,1792]{1,0:T(8,128)(2,1)S(1)} %get-tuple-element.6, bf16[192,1792]{1,0:T(8,128)(2,1)S(1)} %get-tuple-element.4, bf16[192,1024]{1,0:T(8,128)(2,1)} %collective-permute-done, ...), kind=kOutput, calls=%fused_computation.1 | convolution fusion | flops 2838495232 | bytes 10878976 | tf_op jit(solution)/shard_map/dot_general | solution.py:16
  (30 shorter events, 2.7 us)
Async XLA Ops:
  7.2 5.1 %copy-start.2 = (bf16[192,2048]{1,0:T(8,128)(2,1)S(1)}, bf16[192,2048]{1,0:T(8,128)(2,1)}, u32[]{:S(2)}) copy-start(bf16[192,2048]{1,0:T(8,128)(2,1)} %param.4) | copy-start | bytes 2359300
  7.2 46.0 %reduce-scatter.6.cloned.1.call-start = ((), (), s32[]{:S(2)}) async-start(), calls=%async_computation.5 | async-start | bytes 1720320 | tf_op jit(solution)/shard_map/reduce_scatter | solution.py:68
  18.1 69.2 %reduce-scatter.4.cloned.1.call-start = ((), (), s32[]{:S(2)}) async-start(), calls=%async_computation.3 | async-start | bytes 1720320 | tf_op jit(solution)/shard_map/reduce_scatter | solution.py:68
  28.8 93.5 %all-gather.5.cloned.1.call-start = ((), (), s32[]{:S(2)}) async-start(), calls=%async_computation.6 | async-start | bytes 1720320 | tf_op jit(solution)/shard_map/all_gather | solution.py:71
  89.4 67.0 %all-gather.3.cloned.1.call-start = ((), (), s32[]{:S(2)}) async-start(), calls=%async_computation.4 | async-start | bytes 1720320 | tf_op jit(solution)/shard_map/all_gather | solution.py:71
  90.3 141.1 %reduce-scatter.8.cloned.1.call-start = ((), (), s32[]{:S(2)}) async-start(), calls=%async_computation.7 | async-start | bytes 983040 | tf_op jit(solution)/shard_map/reduce_scatter | solution.py:78
  90.6 109.8 %collective-permute-start = (bf16[192,1024]{1,0:T(8,128)(2,1)S(1)}, bf16[192,1024]{1,0:T(8,128)(2,1)}, u32[]{:S(2)}, u32[]{:S(2)}) collective-permute-start(bf16[192,1024]{1,0:T(8,128)(2,1)S(1)} %get-tuple-element.16), channel_id=1, source_target_pairs={{0,1},{1,0},{2,3},{3,2},{4,5},{5,4},{6,7},{7,6},{8,9},{9,8},{10,11... | collective-permute-start | bytes 1179656 | tf_op jit(solution)/shard_map/ppermute | solution.py:52
  122.3 8.4 %copy-start = (bf16[192,3584]{1,0:T(8,128)(2,1)S(1)}, bf16[192,3584]{1,0:T(8,128)(2,1)}, u32[]{:S(2)}) copy-start(bf16[192,3584]{1,0:T(8,128)(2,1)} %all-gather.5.cloned.1.call-done) | copy-start | bytes 4128772
  122.3 48.4 %collective-permute-start.2 = (bf16[192,3584]{1,0:T(8,128)(2,1)}, bf16[192,3584]{1,0:T(8,128)(2,1)}, u32[]{:S(2)}, u32[]{:S(2)}) collective-permute-start(bf16[192,3584]{1,0:T(8,128)(2,1)} %all-gather.5.cloned.1.call-done), channel_id=1, source_target_pairs={{0,1},{1,0},{2,3},{3,2},{4,5},{5,4},{6,7},{7,6},{8,9},{9,8},{10,11... | collective-permute-start | bytes 4128776 | tf_op jit(solution)/shard_map/ppermute | solution.py:52
  156.5 6.0 %copy-start.1 = (bf16[192,3584]{1,0:T(8,128)(2,1)S(1)}, bf16[192,3584]{1,0:T(8,128)(2,1)}, u32[]{:S(2)}) copy-start(bf16[192,3584]{1,0:T(8,128)(2,1)} %all-gather.3.cloned.1.call-done) | copy-start | bytes 4128772
  156.5 6.0 %copy-start.3 = (f32[192,2048]{1,0:T(8,128)S(1)}, f32[192,2048]{1,0:T(8,128)}, u32[]{:S(2)}) copy-start(f32[192,2048]{1,0:T(8,128)} %fusion) | copy-start | bytes 4718596
  156.5 6.0 %copy-start.4 = (f32[192,2048]{1,0:T(8,128)S(1)}, f32[192,2048]{1,0:T(8,128)}, u32[]{:S(2)}) copy-start(f32[192,2048]{1,0:T(8,128)} %fusion.4) | copy-start | bytes 4718596
  169.0 31.3 %collective-permute-start.1 = (bf16[192,3584]{1,0:T(8,128)(2,1)S(1)}, bf16[192,3584]{1,0:T(8,128)(2,1)S(1)}, u32[]{:S(2)}, u32[]{:S(2)}) collective-permute-start(bf16[192,3584]{1,0:T(8,128)(2,1)S(1)} %copy-done.1), channel_id=1, source_target_pairs={{0,1},{1,0},{2,3},{3,2},{4,5},{5,4},{6,7},{7,6},{8,9},{9,8},{10,11... | collective-permute-start | bytes 4128776 | tf_op jit(solution)/shard_map/ppermute | solution.py:52
Sparse Core Ops, SparseCore 0:
  18.2 34.9 reduce-scatter.5
  56.2 31.0 reduce-scatter.3
  89.6 32.6 all-gather.4
  123.7 32.7 all-gather.2
  169.1 22.1 reduce-scatter.7
